TPU v7x, 512 devices: a whole 4x8x8 slice. The times are simulated.
512 devices in a mesh: rep: 16 (over y_hi, x), section: 32 (over y_lo, z, core).
Axes of the slice: x: 4, y: 8 (y_hi: 4, y_lo: 2; y = y_hi * 2 + y_lo), z: 8, core: 2. Of those that a mesh axis runs over, the one named last changes fastest.
Arguments:
- features: bfloat16 [65536, 128], P(('rep', 'section')), may hold values from -6 to 6
- adj_tiles: bfloat16 [65536, 128, 128], P(('rep', 'section')), may hold values from -0.0625 to 0.0625
- tile_rows: int32 [65536], P(('rep', 'section')), may hold values from 0 to 15
- tile_cols: int32 [65536], P(('rep', 'section')), may hold values from 0 to 31
- tile_counts: int32 [512], P(('rep', 'section')), may hold values from 32 to 128, as said below
- weight: bfloat16 [128, 256], replicated, may hold values from -0.5 to 0.5
- out_bias: float32 [256], replicated, may hold values from -3 to 3
Outputs:
- hidden_out: bfloat16 [65536, 256], P(('rep', 'section'))
Inputs may be any that keep to these rules, and one draw needn't show every extreme that they name: `tile_counts`: slots of a device at or beyond its count hold no tile; some device uses all 128 slots in every draw.
All inputs are finite; a program needn't handle non-finite values.
Results may differ from a plain program's by a relative error of at most 0.02.
Values may be sent and summed in bfloat16 or wider, within the bound.
A program may use at most 64 MiB of HBM per device.

v0:
```python
import jax
import jax.numpy as jnp
from jax import lax
from jax.sharding import PartitionSpec as P


def shards(features, adj_tiles, tile_rows, tile_cols, tile_counts, weight, out_bias):
    tile_size = adj_tiles.shape[1]
    slot_count = adj_tiles.shape[0]
    own_rows = features.shape[0]
    channels = features.shape[1]
    rep_count = lax.axis_size("rep")
    row_blocks = rep_count * (own_rows // tile_size)
    gathered = lax.all_gather(features, "section", axis=0, tiled=True)
    sources = gathered.reshape(-1, tile_size, channels)[tile_cols]
    products = jnp.einsum("tij,tjk->tik", adj_tiles, sources, preferred_element_type=jnp.float32)
    products = products.reshape(slot_count, tile_size * channels)
    upper_part = products.astype(jnp.bfloat16)
    lower_part = (products - upper_part.astype(jnp.float32)).astype(jnp.bfloat16)
    live_slots = jnp.arange(slot_count) < tile_counts[0]
    placing = (
        (tile_rows[None, :] == jnp.arange(row_blocks)[:, None]) & live_slots[None, :]
    ).astype(jnp.bfloat16)
    partial_value = jnp.dot(placing, upper_part, preferred_element_type=jnp.float32)
    partial_value = partial_value + jnp.dot(placing, lower_part, preferred_element_type=jnp.float32)
    partial_value = partial_value.reshape(row_blocks * tile_size, channels).astype(jnp.bfloat16)
    combined = lax.psum_scatter(
        jnp.dot(partial_value, weight, preferred_element_type=jnp.float32).astype(jnp.bfloat16),
        "rep",
        scatter_dimension=0,
        tiled=True,
    ).astype(jnp.float32)
    return jax.nn.relu(combined + out_bias).astype(jnp.bfloat16)


def solution(mesh):
    in_specs = (
        P(("rep", "section"), None),
        P(("rep", "section"), None, None),
        P(("rep", "section")),
        P(("rep", "section")),
        P(("rep", "section")),
        P(),
        P(),
    )
    out_specs = P(("rep", "section"), None)
    return jax.shard_map(shards, mesh=mesh, in_specs=in_specs, out_specs=out_specs, check_vma=False)
```

profile of v0, /device:TPU:1, one launch (start us, length us, event | category | flops | bytes accessed | tf_op | source)
XLA Modules:
  0.0 210.9 jit_solution(17311236306386423818)
XLA Ops:
  6.5 0.0 copy-start
  6.5 0.0 all-gather.2.cloned.1.call-start
  6.5 0.7 all-gather.2.cloned.1.call-update
  7.3 0.0 reduce-scatter.2.cloned.1.call-start
  8.0 0.7 compare_select_fusion
  8.6 73.6 %all-gather.2.cloned.1.call-done = bf16[4096,128]{1,0:T(8,128)(2,1)} async-done(((bf16[128,128]{1,0:T(8,128)(2,1)}), bf16[4096,128]{1,0:T(8,128)(2,1)}) %all-gather.2.cloned.1.call-update) | async-done | bytes 1048592 | tf_op jit(solution)/shard_map/all_gather | solution.py:14
  82.2 4.3 %gather_fusion = bf16[128,128,128]{2,1,0:T(8,128)(2,1)} fusion(bf16[32,128,128]{2,1,0:T(8,128)(2,1)} %bitcast.17, s32[1024]{0:T(1024)S(1)} %pad_clamp_fusion), kind=kCustom, calls=%fused_computation | custom fusion | bytes 8389120 | tf_op jit(solution)/shard_map/gather | solution.py:15
  86.5 9.8 %convolution_bitcast_fusion = f32[128,128,128]{1,2,0:T(8,128)} fusion(bf16[128,128,128]{2,1,0:T(8,128)(2,1)} %gather_fusion, bf16[128,128,128]{2,1,0:T(8,128)(2,1)} %param.8), kind=kOutput, calls=%fused_computation.6 | convolution fusion | flops 536870912 | bytes 16777216 | tf_op jit(solution)/shard_map/tij,tjk->tik/dot_general | solution.py:16
  96.3 9.3 %copy.9 = f32[128,128,128]{0,2,1:T(8,128)} copy(f32[128,128,128]{1,2,0:T(8,128)} %convolution_bitcast_fusion) | data formatting | bytes 16777216 | tf_op jit(solution)/shard_map/tij,tjk->tik/dot_general | solution.py:16
  105.6 0.0 copy-start.1
  105.6 4.0 %fusion.1 = (bf16[128,16384]{0,1:T(8,128)(2,1)S(1)}, bf16[128,16384]{0,1:T(8,128)(2,1)S(1)}) fusion(f32[128,128,128]{0,2,1:T(8,128)} %copy.9), kind=kLoop, calls=%fused_computation.5 | loop fusion | flops 8388608 | bytes 16777216 | tf_op jit(solution)/shard_map/convert_element_type | solution.py:19
  109.6 0.0 copy-done.1
  109.6 1.2 fusion.4
  110.8 0.0 copy-start.2
  110.8 1.2 fusion
  112.0 0.3 convert_element_type.29
  112.3 0.0 copy-done
  112.3 1.4 convolution_convert_fusion
  113.7 0.0 reduce-scatter.2.cloned.1.call-update
  113.7 88.8 %reduce-scatter.2.cloned.1.call-done = bf16[128,256]{1,0:T(8,128)(2,1)} async-done(((bf16[2048,256]{1,0:T(8,128)(2,1)}), bf16[128,256]{1,0:T(8,128)(2,1)}) %reduce-scatter.2.cloned.1.call-update) | async-done | bytes 65552 | tf_op jit(solution)/shard_map/reduce_scatter | solution.py:27
  202.5 0.0 copy-done.2
  202.5 1.5 maximum_convert_fusion
  (2 shorter events, 0.0 us)
Async XLA Ops:
  6.5 105.8 %copy-start = (bf16[128,256]{1,0:T(8,128)(2,1)S(1)}, bf16[128,256]{1,0:T(8,128)(2,1)}, u32[]{:S(2)}) copy-start(bf16[128,256]{1,0:T(8,128)(2,1)} %param.12) | copy-start | bytes 196612
  6.5 75.7 %all-gather.2.cloned.1.call-start = ((), (), s32[]{:S(2)}) async-start(), calls=%async_computation.1 | async-start | bytes 1081344 | tf_op jit(solution)/shard_map/all_gather | solution.py:14
  7.3 195.3 %reduce-scatter.2.cloned.1.call-start = ((), (), s32[]{:S(2)}) async-start(), calls=%async_computation.2 | async-start | bytes 1114112 | tf_op jit(solution)/shard_map/reduce_scatter | solution.py:27
  105.6 4.0 %copy-start.1 = (s32[128]{0:T(128)S(1)}, s32[128]{0:T(128)}, u32[]{:S(2)}) copy-start(s32[128]{0:T(128)} %param.9) | copy-start | bytes 1540
  110.8 91.7 %copy-start.2 = (f32[256]{0:T(256)S(1)}, f32[256]{0:T(256)}, u32[]{:S(2)}) copy-start(f32[256]{0:T(256)} %param.13) | copy-start | bytes 3076
Sparse Core Ops, SparseCore 0:
  9.5 72.6 all-gather.1
  113.8 88.6 reduce-scatter.1
where the time goes:
time: 212 us; the launch traced here: 211 us
  waiting for transfers between devices  163 us (77%)
  between operations  14.1 us (7%)
  local copies, waits for them, and re-layouts  13.9 us (7%)
  matrix products  13.6 us (6%)
  other arithmetic  6.19 us (3%)
    reduce_scatter x1, waiting for transfers between devices, shards(): lax.psum_scatter(jnp.dot(partial_value, weight, preferred_element_type=jn...  88.8 us
    all_gather x1, waiting for transfers between devices, shards(): gathered = lax.all_gather(features, 'section', axis=0, tiled=True)  73.6 us
    dot_general x1, matrix products, shards(): jnp.einsum('tij,tjk->tik', adj_tiles, sources, preferred_element_type=jnp...  9.77 us
    dot_general x1, local copies, waits for them, and re-layouts, shards(): jnp.einsum('tij,tjk->tik', adj_tiles, sources, preferred_element_type=jnp...  9.32 us
    gather x1, local copies, waits for them, and re-layouts, shards(): sources = gathered.reshape(-1, tile_size, channels)[tile_cols]  4.27 us
  transfers between devices with their start and end apart: 2, of which 2 were waited for; matrix products, arithmetic and copies ran while one was open for 0% of the time, Pallas kernels for 0%

commit v1 on v0

v1 whole, which is shorter than its diff:
```python
import jax
import jax.numpy as jnp
from jax import lax
from jax.experimental import pallas as pl
from jax.experimental.pallas import tpu as pltpu
from jax.sharding import PartitionSpec as P

MESH = pl.DeviceIdType.MESH
NX, NY, NZ = 4, 4, 8
RELAYS = NZ // 2 - 1

HALF = 64


def kernel(
    features, adjacency, rows_in, cols_in, count_in, weight_in, bias_in, out_ref,
    rows_ref, cols_ref, count_ref, weight, bias,
    slab, tiles, sums, plan_v, plan, outbox, inbox_x, relay_y, inbox_y,
    local_sem, send_z, recv_z, send_y, recv_y, send_c, recv_c, send_px, recv_px, send_py, recv_py,
):
    rep, section = lax.axis_index("rep"), lax.axis_index("section")
    yh, x = rep // NX, rep % NX
    y, z, core = section // (2 * NZ), (section // 2) % NZ, section % 2
    z_up = y * 2 * NZ + ((z + 1) % NZ) * 2 + core
    z_down = y * 2 * NZ + ((z + NZ - 1) % NZ) * 2 + core
    partner = (1 - y) * 2 * NZ + z * 2 + core
    sibling = section + 1 - 2 * core

    def x_peer(step):
        return yh * NX + (x + step) % NX

    def y_peer(step):
        return ((yh + step) % NY) * NX + x

    def base(at):
        return (at * 2 + core) * 4

    own_rows = slab.at[pl.ds(base(z) + 1, 2)]
    small = [
        pltpu.make_async_copy(source, target, local_sem.at[3 + i])
        for i, (source, target) in enumerate(
            ((rows_in, rows_ref), (cols_in, cols_ref), (count_in, count_ref), (weight_in, weight), (bias_in, bias))
        )
    ]
    tile_copy = pltpu.make_async_copy(adjacency, tiles, local_sem.at[0])
    own_copy = pltpu.make_async_copy(features, own_rows, local_sem.at[1])
    own_copy.start()
    for copy in small:
        copy.start()
    tile_copy.start()

    barrier = pltpu.get_barrier_semaphore()
    for peer in (z_up, z_down, partner, sibling):
        pl.semaphore_signal(barrier, inc=1, device_id={"section": peer}, device_id_type=MESH)
    for step in range(1, NX):
        pl.semaphore_signal(barrier, inc=1, device_id={"rep": x_peer(step)}, device_id_type=MESH)
    for step in range(1, NY):
        pl.semaphore_signal(barrier, inc=1, device_id={"rep": y_peer(step)}, device_id_type=MESH)
    own_copy.wait()
    pl.semaphore_wait(barrier, 4 + NX - 1 + NY - 1)

    sent = []

    def piece(at, begin, count):
        return slab.at[pl.ds(base(at) + begin, count)]

    def push(source, target, send, recv, peer):
        copy = pltpu.make_async_remote_copy(
            src_ref=source, dst_ref=target, send_sem=send, recv_sem=recv,
            device_id=peer, device_id_type=MESH,
        )
        copy.start()
        sent.append(copy)
        return copy

    def along_z(way, step, kind):
        at = (z - step + NZ) % NZ if way == 0 else (z + step) % NZ
        last = step == RELAYS
        if kind == 0:
            ref = piece(at, 1 + way, 1) if last else piece(at, 1, 2)
        elif last:
            ref = slab.at[base(at), pl.ds(way * (HALF // 2), HALF // 2)]
        else:
            ref = piece(at, 0, 1)
        return push(ref, ref, send_z.at[way, step, kind], recv_z.at[way, step, kind], {"section": (z_up, z_down)[way]})

    def to_partner(at, slot, begin, target):
        return push(piece(at, begin, 1), piece(at, target, 1), send_y.at[slot], recv_y.at[slot], {"section": partner})

    def to_sibling(at, slot, part):
        ref = piece(at, *((1, 2), (0, 1), (3, 1))[part])
        return push(ref, ref, send_c.at[slot, part], recv_c.at[slot, part], {"section": sibling})

    def origin(way, step):
        return (z - step - 1 + NZ) % NZ if way == 0 else (z + step + 1) % NZ

    def slot_of(way, step):
        return 1 + 2 * step + way

    first = to_partner(z, NZ, 1, 0)
    wide = [along_z(0, 0, 0), along_z(1, 0, 0)]
    lower = [(z, 0, to_partner(z, 0, 2, 3))]
    siblings = [to_sibling(z, 0, 0)]

    for copy in small:
        copy.wait()
    lane = lax.broadcasted_iota(jnp.int32, (128, 128), 1)
    down = lax.broadcasted_iota(jnp.int32, (128, 128), 0)
    row_across = jnp.broadcast_to(rows_ref[...], (128, 128))
    row_across = jnp.where(lane < jnp.broadcast_to(count_ref[...], (128, 128)), row_across, NX * NY)
    key_across = row_across * 128 + lane
    key_down = key_across.T
    rank = jnp.sum((key_down < key_across).astype(jnp.int32), axis=0, keepdims=True)
    rank_down = jnp.broadcast_to(rank, (128, 128)).T
    col_across = jnp.broadcast_to(cols_ref[...], (128, 128))
    info_across = lane + col_across * 128 + row_across * 4096
    info_down = info_across.T
    row_down = key_down // 128
    order = jnp.sum(jnp.where(rank_down == lane, info_down, 0), axis=0, keepdims=True)
    ends = jnp.sum((row_down <= lane).astype(jnp.int32), axis=0, keepdims=True)
    used = jnp.sum((row_down == lane).astype(jnp.int32), axis=0, keepdims=True)
    line = lax.broadcasted_iota(jnp.int32, (8, 128), 0)
    plan_v[...] = jnp.where(line == 0, order, jnp.where(line == 1, ends, used))
    plan_copy = pltpu.make_async_copy(plan_v, plan, local_sem.at[2])
    plan_copy.start()

    first.wait_recv()
    narrow = [along_z(0, 0, 1), along_z(1, 0, 1)]
    siblings.append(to_sibling(z, 0, 1))
    for step in range(RELAYS):
        arrived, wide_next, narrow_next = lower, [], []
        lower = []
        for way in range(2):
            wide[way].wait_recv()
            wide_next.append(along_z(way, step + 1, 0))
            at, slot = origin(way, step), slot_of(way, step)
            lower.append((at, slot, to_partner(at, slot, 2, 3)))
            siblings.append(to_sibling(at, slot, 0))
        for way in range(2):
            narrow[way].wait_recv()
            narrow_next.append(along_z(way, step + 1, 1))
            siblings.append(to_sibling(origin(way, step), slot_of(way, step), 1))
        for at, slot, copy in arrived:
            copy.wait_recv()
            siblings.append(to_sibling(at, slot, 2))
        wide, narrow = wide_next, narrow_next
    far = (z + NZ // 2) % NZ
    far_slot = NZ - 1
    wide[1].wait_recv()
    lower.append((far, far_slot, to_partner(far, far_slot, 2, 3)))
    wide[0].wait_recv()
    siblings.append(to_sibling(far, far_slot, 0))
    for way in range(2):
        narrow[way].wait_recv()
    siblings.append(to_sibling(far, far_slot, 1))
    for at, slot, copy in lower:
        copy.wait_recv()
        siblings.append(to_sibling(at, slot, 2))
    plan_copy.wait()
    tile_copy.wait()
    for copy in siblings:
        copy.wait_recv()

    def step_of(k, carry):
        total, row_before = carry
        info = plan[0, k]
        slot, col, row = info & 127, (info >> 7) & 31, info >> 12
        other = (col >> 4) ^ y
        at = (col & 15) * 4
        source = jnp.concatenate([slab[at + 1 - other], slab[at + 2 + other]], axis=0)
        product = jnp.dot(tiles[slot], source, preferred_element_type=jnp.float32)
        total = total * jnp.where(row == row_before, 1.0, 0.0) + product
        sums[k] = total
        return total, row

    lax.fori_loop(0, 128, step_of, (jnp.zeros((128, 128), jnp.float32), jnp.int32(-1)), unroll=4)

    def partial_of(q):
        end = jnp.maximum(plan[1, q] - 1, 0)
        return (sums[end] * jnp.minimum(plan[2, q], 1).astype(jnp.float32)).astype(jnp.bfloat16)

    hops_y = (2, 1, 3, 0)
    sends = {}
    for jy in hops_y:
        yq = (yh + jy) % NY
        for jx in (2, 1, 3):
            outbox[jy, jx] = partial_of(yq * NX + (x + jx) % NX)
            sends[jy, jx] = push(
                outbox.at[jy, jx], inbox_x.at[jy, jx - 1], send_px.at[jy, jx - 1], recv_px.at[jy, jx - 1], {"rep": x_peer(jx)}
            )
        outbox[jy, 0] = partial_of(yq * NX + x)
    total = None
    second = {}
    for jy in hops_y:
        total = outbox[jy, 0].astype(jnp.float32)
        for jx in (1, 3, 2):
            sends[jy, jx].wait_recv()
            total = total + inbox_x[jy, jx - 1].astype(jnp.float32)
        if jy:
            relay_y[jy - 1] = total.astype(jnp.bfloat16)
            second[jy] = push(
                relay_y.at[jy - 1], inbox_y.at[jy - 1], send_py.at[jy - 1], recv_py.at[jy - 1], {"rep": y_peer(jy)}
            )
    for jy in (1, 3, 2):
        second[jy].wait_recv()
        total = total + inbox_y[jy - 1].astype(jnp.float32)
    high = total.astype(jnp.bfloat16)
    low = (total - high.astype(jnp.float32)).astype(jnp.bfloat16)
    hidden = jnp.dot(high, weight[...], preferred_element_type=jnp.float32)
    hidden = hidden + jnp.dot(low, weight[...], preferred_element_type=jnp.float32)
    out_ref[...] = jnp.maximum(hidden + bias[...], 0.0).astype(jnp.bfloat16)
    for copy in sent:
        copy.wait_send()


def shards(features, adj_tiles, tile_rows, tile_cols, tile_counts, weight, out_bias):
    vmem = pl.BlockSpec(memory_space=pltpu.VMEM)
    anywhere = pl.BlockSpec(memory_space=pl.ANY)
    dma = pltpu.SemaphoreType.DMA
    bf16 = jnp.bfloat16
    return pl.pallas_call(
        kernel,
        out_shape=jax.ShapeDtypeStruct((128, 256), bf16),
        in_specs=[anywhere] * 7,
        out_specs=vmem,
        scratch_shapes=[
            pltpu.VMEM((1, 128), jnp.int32),
            pltpu.VMEM((1, 128), jnp.int32),
            pltpu.VMEM((1, 1), jnp.int32),
            pltpu.VMEM((128, 256), bf16),
            pltpu.VMEM((1, 256), jnp.float32),
            pltpu.VMEM((NZ * 2 * 4, HALF, 128), bf16),
            pltpu.VMEM((128, 128, 128), bf16),
            pltpu.VMEM((128, 128, 128), jnp.float32),
            pltpu.VMEM((8, 128), jnp.int32),
            pltpu.SMEM((8, 128), jnp.int32),
            pltpu.VMEM((NY, NX, 128, 128), bf16),
            pltpu.VMEM((NY, NX - 1, 128, 128), bf16),
            pltpu.VMEM((NY - 1, 128, 128), bf16),
            pltpu.VMEM((NY - 1, 128, 128), bf16),
            dma((8,)),
            dma((2, RELAYS + 1, 2)),
            dma((2, RELAYS + 1, 2)),
            dma((NZ + 1,)),
            dma((NZ + 1,)),
            dma((NZ, 3)),
            dma((NZ, 3)),
            dma((NY, NX - 1)),
            dma((NY, NX - 1)),
            dma((NY - 1,)),
            dma((NY - 1,)),
        ],
        compiler_params=pltpu.CompilerParams(
            collective_id=0, has_side_effects=True, vmem_limit_bytes=60 * 1024 * 1024
        ),
        cost_estimate=pl.CostEstimate(flops=2 * 128**4, bytes_accessed=128**3 * 2, transcendentals=0),
        name="layer",
    )(features.reshape(2, HALF, 128), adj_tiles, tile_rows.reshape(1, 128), tile_cols.reshape(1, 128), tile_counts.reshape(1, 1), weight, out_bias.reshape(1, 256))


def solution(mesh):
    in_specs = (
        P(("rep", "section"), None),
        P(("rep", "section"), None, None),
        P(("rep", "section")),
        P(("rep", "section")),
        P(("rep", "section")),
        P(),
        P(),
    )
    out_specs = P(("rep", "section"), None)
    return jax.shard_map(shards, mesh=mesh, in_specs=in_specs, out_specs=out_specs, check_vma=False)
```

time: 212 us -> 52.1 us (0.25)
  waiting for transfers between devices: 163 us -> 0 us
  Pallas kernels: 0 us -> 49.8 us
  matrix products: 13.6 us -> 0 us
  between operations: 14.1 us -> 0.66 us
  local copies, waits for them, and re-layouts: 13.9 us -> 1.47 us
  other arithmetic: 6.19 us -> 0 us
    reduce_scatter x1 -> x0, waiting for transfers between devices: 88.8 us -> none  [shards(): lax.psum_scatter(jnp.dot(partial_value, weight, preferred_element_type=jn...]
    all_gather x1 -> x0, waiting for transfers between devices: 73.6 us -> none  [shards(): gathered = lax.all_gather(features, 'section', axis=0, tiled=True)]
    pallas_call x0 -> x1, Pallas kernels: none -> 49.8 us  [shards(): pl.pallas_call(kernel, out_shape=jax.ShapeDtypeStruct((128, 256), bf16),...]
    dot_general x4 -> x0, matrix products: 13.6 us -> none  [the longest x1 9.77 us: shards(): jnp.einsum('tij,tjk->tik', adj_tiles, sources, preferred_element_type=jnp...]
    dot_general x1 -> x0, local copies, waits for them, and re-layouts: 9.32 us -> none  [shards(): jnp.einsum('tij,tjk->tik', adj_tiles, sources, preferred_element_type=jnp...]
    convert_element_type x2 -> x0, other arithmetic: 5.52 us -> none  [the longest x1 4.03 us: shards(): (products - upper_part.astype(jnp.float32)).astype(jnp.bfloat16)]
    gather x1 -> x0, local copies, waits for them, and re-layouts: 4.27 us -> none  [shards(): sources = gathered.reshape(-1, tile_size, channels)[tile_cols]]
  transfers between devices with their start and end apart: 2 -> 0, of which waited for: 2 -> 0; matrix products, arithmetic and copies ran while one was open for 0% -> 0% of each run, Pallas kernels for 0% -> 0%
where the time goes in v1:
time: 52.1 us; the launch traced here: 52 us
  Pallas kernels  49.8 us (96%)
  local copies, waits for them, and re-layouts  1.47 us (3%)
  between operations  0.66 us (1%)
    pallas_call x1, Pallas kernels, shards(): pl.pallas_call(kernel, out_shape=jax.ShapeDtypeStruct((128, 256), bf16),...  49.8 us
    unnamed x1, local copies, waits for them, and re-layouts  1.47 us

profile of v1, /device:TPU:1, one launch (start us, length us, event | category | flops | bytes accessed | tf_op | source)
XLA Modules:
  0.0 52.0 jit_solution(7226784446940809067)
XLA Ops:
  0.7 49.8 %layer.1 = bf16[128,256]{1,0:T(8,128)(2,1)} custom-call(bf16[2,64,128]{2,1,0:T(8,128)(2,1)} %bitcast.6, bf16[128,128,128]{2,1,0:T(8,128)(2,1)} %adjacency.1, s32[1,128]{1,0:T(1,128)} %bitcast.8, s32[1,128]{1,0:T(1,128)} %bitcast.9, s32[1,1]{1,0:T(1,128)} %bitcast.5.count_in, bf16[128,256]{1,0:T(8,128)(2,1)} %weight_in.1, f32[1,256]{1,0:T(1,128)} %bitcast.7), custom_call_target="tpu_custom_call" | custom-call | flops 536870912 | bytes 4194304 | tf_op jit(solution)/shard_map/layer/pallas_call | solution.py:221
  50.5 1.5 %copy.10 = bf16[128,256]{1,0:T(8,128)(2,1)} copy(bf16[128,256]{1,0:T(8,128)(2,1)} %layer.1) | data formatting | bytes 131072

commit v2 on v1

v2 whole, which is shorter than its diff:
```python
import jax
import jax.numpy as jnp
from jax import lax
from jax.experimental import pallas as pl
from jax.experimental.pallas import tpu as pltpu
from jax.sharding import PartitionSpec as P

MESH = pl.DeviceIdType.MESH
NX, NY, NZ = 4, 4, 8
PAIRS = 72


def kernel(
    features, adjacency, rows_in, cols_in, count_in, weight_in, bias_in, out_ref,
    rows_ref, cols_ref, count_ref, weight, bias,
    slab, tiles, sums, plan_v, plan, outbox, inbox_x, relay_y, inbox_y,
    local_sem, send_z, recv_z, send_y, recv_y, send_c, recv_c, send_px, recv_px, send_py, recv_py,
):
    rep, section = lax.axis_index("rep"), lax.axis_index("section")
    yh, x = rep // NX, rep % NX
    y, z, core = section // (2 * NZ), (section // 2) % NZ, section % 2
    partner = (1 - y) * 2 * NZ + z * 2 + core
    sibling = section + 1 - 2 * core

    def at_z(step):
        return y * 2 * NZ + ((z + step + NZ) % NZ) * 2 + core

    def x_peer(step):
        return yh * NX + (x + step) % NX

    def y_peer(step):
        return ((yh + step) % NY) * NX + x

    def block(owner):
        return slab.at[owner + 1]

    small = [
        pltpu.make_async_copy(source, target, local_sem.at[3 + i])
        for i, (source, target) in enumerate(
            ((rows_in, rows_ref), (cols_in, cols_ref), (count_in, count_ref), (weight_in, weight), (bias_in, bias))
        )
    ]
    tile_copy = pltpu.make_async_copy(adjacency, tiles, local_sem.at[0])
    own_copy = pltpu.make_async_copy(features, block(section), local_sem.at[1])
    own_copy.start()
    for copy in small:
        copy.start()
    tile_copy.start()

    barrier = pltpu.get_barrier_semaphore()
    for peer in [at_z(step) for step in range(1, NZ)] + [partner, sibling]:
        pl.semaphore_signal(barrier, inc=1, device_id={"section": peer}, device_id_type=MESH)
    for step in range(1, NX):
        pl.semaphore_signal(barrier, inc=1, device_id={"rep": x_peer(step)}, device_id_type=MESH)
    for step in range(1, NY):
        pl.semaphore_signal(barrier, inc=1, device_id={"rep": y_peer(step)}, device_id_type=MESH)
    own_copy.wait()
    pl.semaphore_wait(barrier, NZ + 1 + NX - 1 + NY - 1)

    sent = []

    def push(source, target, send, recv, peer):
        copy = pltpu.make_async_remote_copy(
            src_ref=source, dst_ref=target, send_sem=send, recv_sem=recv,
            device_id=peer, device_id_type=MESH,
        )
        copy.start()
        sent.append(copy)
        return copy

    def along_z(step):
        ref = block(section)
        return push(ref, ref, send_z.at[step + 3], recv_z.at[step + 3], {"section": at_z(step)})

    def to_partner(owner, slot):
        return push(block(owner), block(owner), send_y.at[slot], recv_y.at[slot], {"section": partner})

    def to_sibling(owner, slot):
        return push(block(owner), block(owner), send_c.at[slot], recv_c.at[slot], {"section": sibling})

    near = (1, -1, 2, -2, 3, -3, 4)
    along = {step: along_z(step) for step in near}
    across = [(section, to_partner(section, 0))]
    siblings = [to_sibling(section, 0)]

    slab[0] = jnp.zeros((128, 128), jnp.bfloat16)
    for copy in small:
        copy.wait()
    lane = lax.broadcasted_iota(jnp.int32, (128, 128), 1)
    down = lax.broadcasted_iota(jnp.int32, (128, 128), 0)
    row_across = jnp.broadcast_to(rows_ref[...], (128, 128))
    row_across = jnp.where(lane < jnp.broadcast_to(count_ref[...], (128, 128)), row_across, NX * NY)
    row_down = row_across.T
    same = row_down == row_across
    earlier = jnp.sum((same & (down < lane)).astype(jnp.int32), axis=0, keepdims=True)
    count = jnp.sum(same.astype(jnp.int32), axis=0, keepdims=True)
    places = 1 + jnp.where(earlier == count - 1, count & 1, 0)
    places_down = jnp.broadcast_to(places, (128, 128)).T
    place = jnp.sum(jnp.where(row_down < row_across, places_down, 0), axis=0, keepdims=True) + earlier
    place_down = jnp.broadcast_to(place, (128, 128)).T
    col_across = jnp.broadcast_to(cols_ref[...], (128, 128))
    info_down = (lane + (col_across + 1) * 128 + row_across * 8192).T
    first = jnp.sum(jnp.where(place_down == 2 * lane, info_down, 0), axis=0, keepdims=True)
    second = jnp.sum(jnp.where(place_down == 2 * lane + 1, info_down, 0), axis=0, keepdims=True)
    ends = jnp.sum(jnp.where(row_down <= lane, places_down, 0), axis=0, keepdims=True)
    used = jnp.sum((row_down == lane).astype(jnp.int32), axis=0, keepdims=True)
    line = lax.broadcasted_iota(jnp.int32, (8, 128), 0)
    plan_v[...] = jnp.where(line == 0, first, jnp.where(line == 1, second, jnp.where(line == 2, ends, used)))
    plan_copy = pltpu.make_async_copy(plan_v, plan, local_sem.at[2])
    plan_copy.start()

    for slot, step in enumerate(near):
        along[step].wait_recv()
        owner = at_z(-step)
        across.append((owner, to_partner(owner, slot + 1)))
        siblings.append(to_sibling(owner, slot + 1))
    for slot, (owner, copy) in enumerate(across):
        copy.wait_recv()
        siblings.append(to_sibling((owner + 2 * NZ) % (4 * NZ), NZ + slot))
    plan_copy.wait()
    tile_copy.wait()
    for copy in siblings:
        copy.wait_recv()

    def step_of(k, carry):
        total, row_before = carry
        one, two = plan[0, k], plan[1, k]
        row = one >> 13
        pair = jnp.concatenate([tiles[one & 127], tiles[two & 127]], axis=1)
        source = jnp.concatenate([slab[(one >> 7) & 63], slab[(two >> 7) & 63]], axis=0)
        product = jnp.dot(pair, source, preferred_element_type=jnp.float32)
        total = total * jnp.where(row == row_before, 1.0, 0.0) + product
        sums[k] = total
        return total, row

    lax.fori_loop(0, PAIRS, step_of, (jnp.zeros((128, 128), jnp.float32), jnp.int32(-1)), unroll=24)

    def partial_of(q):
        end = jnp.maximum((plan[2, q] >> 1) - 1, 0)
        return (sums[end] * jnp.minimum(plan[3, q], 1).astype(jnp.float32)).astype(jnp.bfloat16)

    hops_y = (2, 1, 3, 0)
    sends = {}
    for jy in hops_y:
        yq = (yh + jy) % NY
        for jx in (2, 1, 3):
            outbox[jy, jx] = partial_of(yq * NX + (x + jx) % NX)
            sends[jy, jx] = push(
                outbox.at[jy, jx], inbox_x.at[jy, jx - 1], send_px.at[jy, jx - 1], recv_px.at[jy, jx - 1], {"rep": x_peer(jx)}
            )
        outbox[jy, 0] = partial_of(yq * NX + x)
    total = None
    onward = {}
    for jy in hops_y:
        total = outbox[jy, 0].astype(jnp.float32)
        for jx in (1, 3, 2):
            sends[jy, jx].wait_recv()
            total = total + inbox_x[jy, jx - 1].astype(jnp.float32)
        if jy:
            relay_y[jy - 1] = total.astype(jnp.bfloat16)
            onward[jy] = push(
                relay_y.at[jy - 1], inbox_y.at[jy - 1], send_py.at[jy - 1], recv_py.at[jy - 1], {"rep": y_peer(jy)}
            )
    for jy in (1, 3, 2):
        onward[jy].wait_recv()
        total = total + inbox_y[jy - 1].astype(jnp.float32)
    high = total.astype(jnp.bfloat16)
    low = (total - high.astype(jnp.float32)).astype(jnp.bfloat16)
    hidden = jnp.dot(high, weight[...], preferred_element_type=jnp.float32)
    hidden = hidden + jnp.dot(low, weight[...], preferred_element_type=jnp.float32)
    out_ref[...] = jnp.maximum(hidden + bias[...], 0.0).astype(jnp.bfloat16)
    for copy in sent:
        copy.wait_send()


def shards(features, adj_tiles, tile_rows, tile_cols, tile_counts, weight, out_bias):
    vmem = pl.BlockSpec(memory_space=pltpu.VMEM)
    anywhere = pl.BlockSpec(memory_space=pl.ANY)
    dma = pltpu.SemaphoreType.DMA
    bf16 = jnp.bfloat16
    return pl.pallas_call(
        kernel,
        out_shape=jax.ShapeDtypeStruct((128, 256), bf16),
        in_specs=[anywhere] * 7,
        out_specs=vmem,
        scratch_shapes=[
            pltpu.VMEM((1, 128), jnp.int32),
            pltpu.VMEM((1, 128), jnp.int32),
            pltpu.VMEM((1, 1), jnp.int32),
            pltpu.VMEM((128, 256), bf16),
            pltpu.VMEM((1, 256), jnp.float32),
            pltpu.VMEM((4 * NZ + 1, 128, 128), bf16),
            pltpu.VMEM((128, 128, 128), bf16),
            pltpu.VMEM((PAIRS, 128, 128), jnp.float32),
            pltpu.VMEM((8, 128), jnp.int32),
            pltpu.SMEM((8, 128), jnp.int32),
            pltpu.VMEM((NY, NX, 128, 128), bf16),
            pltpu.VMEM((NY, NX - 1, 128, 128), bf16),
            pltpu.VMEM((NY - 1, 128, 128), bf16),
            pltpu.VMEM((NY - 1, 128, 128), bf16),
            dma((8,)),
            dma((NZ,)),
            dma((NZ,)),
            dma((NZ,)),
            dma((NZ,)),
            dma((2 * NZ,)),
            dma((2 * NZ,)),
            dma((NY, NX - 1)),
            dma((NY, NX - 1)),
            dma((NY - 1,)),
            dma((NY - 1,)),
        ],
        compiler_params=pltpu.CompilerParams(
            collective_id=0, has_side_effects=True, vmem_limit_bytes=60 * 1024 * 1024
        ),
        cost_estimate=pl.CostEstimate(flops=2 * 128**4, bytes_accessed=128**3 * 2, transcendentals=0),
        name="layer",
    )(features, adj_tiles, tile_rows.reshape(1, 128), tile_cols.reshape(1, 128), tile_counts.reshape(1, 1), weight, out_bias.reshape(1, 256))


def solution(mesh):
    in_specs = (
        P(("rep", "section"), None),
        P(("rep", "section"), None, None),
        P(("rep", "section")),
        P(("rep", "section")),
        P(("rep", "section")),
        P(),
        P(),
    )
    out_specs = P(("rep", "section"), None)
    return jax.shard_map(shards, mesh=mesh, in_specs=in_specs, out_specs=out_specs, check_vma=False)
```

time: 52.1 us -> 43 us (0.83)
  Pallas kernels: 49.8 us -> 40.7 us
    pallas_call x1, Pallas kernels: 49.8 us -> 40.7 us  [shards(): pl.pallas_call(kernel, out_shape=jax.ShapeDtypeStruct((128, 256), bf16),...]
where the time goes in v2:
time: 43 us; the launch traced here: 42.9 us
  Pallas kernels  40.7 us (95%)
  local copies, waits for them, and re-layouts  1.47 us (3%)
  between operations  0.66 us (2%)
    pallas_call x1, Pallas kernels, shards(): pl.pallas_call(kernel, out_shape=jax.ShapeDtypeStruct((128, 256), bf16),...  40.7 us
    unnamed x1, local copies, waits for them, and re-layouts  1.47 us

profile of v2, /device:TPU:1, one launch (start us, length us, event | category | flops | bytes accessed | tf_op | source)
XLA Modules:
  0.0 42.9 jit_solution(5807251385800586594)
XLA Ops:
  0.7 40.7 %layer.1 = bf16[128,256]{1,0:T(8,128)(2,1)} custom-call(bf16[128,128]{1,0:T(8,128)(2,1)} %features.1, bf16[128,128,128]{2,1,0:T(8,128)(2,1)} %adjacency.1, s32[1,128]{1,0:T(1,128)} %bitcast.6, s32[1,128]{1,0:T(1,128)} %bitcast.7, s32[1,1]{1,0:T(1,128)} %bitcast.4.count_in, bf16[128,256]{1,0:T(8,128)(2,1)} %weight_in.1, f32[1,256]{1,0:T(1,128)} %bitcast.5), custom_call_target="tpu_custom_call" | custom-call | flops 536870912 | bytes 4194304 | tf_op jit(solution)/shard_map/layer/pallas_call | solution.py:181
  41.4 1.5 %copy.10 = bf16[128,256]{1,0:T(8,128)(2,1)} copy(bf16[128,256]{1,0:T(8,128)(2,1)} %layer.1) | data formatting | bytes 131072

commit v3 on v2

--- a/solution.py
+++ b/solution.py
@@ -7,14 +7,16 @@
 
 MESH = pl.DeviceIdType.MESH
 NX, NY, NZ = 4, 4, 8
+X_FIRST = 96
 PAIRS = 72
 
 
 def kernel(
     features, adjacency, rows_in, cols_in, count_in, weight_in, bias_in, out_ref,
     rows_ref, cols_ref, count_ref, weight, bias,
-    slab, tiles, sums, plan_v, plan, outbox, inbox_x, relay_y, inbox_y,
+    slab, tiles, sums, plan_v, plan, outbox, inbox_x, relay_y, inbox_y, inbox_q, relay_x, inbox_r,
     local_sem, send_z, recv_z, send_y, recv_y, send_c, recv_c, send_px, recv_px, send_py, recv_py,
+    send_pq, recv_pq, send_pr, recv_pr,
 ):
     rep, section = lax.axis_index("rep"), lax.axis_index("section")
     yh, x = rep // NX, rep % NX
@@ -139,31 +141,50 @@
         end = jnp.maximum((plan[2, q] >> 1) - 1, 0)
         return (sums[end] * jnp.minimum(plan[3, q], 1).astype(jnp.float32)).astype(jnp.bfloat16)
 
-    hops_y = (2, 1, 3, 0)
-    sends = {}
-    for jy in hops_y:
-        yq = (yh + jy) % NY
-        for jx in (2, 1, 3):
-            outbox[jy, jx] = partial_of(yq * NX + (x + jx) % NX)
-            sends[jy, jx] = push(
-                outbox.at[jy, jx], inbox_x.at[jy, jx - 1], send_px.at[jy, jx - 1], recv_px.at[jy, jx - 1], {"rep": x_peer(jx)}
-            )
-        outbox[jy, 0] = partial_of(yq * NX + x)
-    total = None
-    onward = {}
-    for jy in hops_y:
-        total = outbox[jy, 0].astype(jnp.float32)
-        for jx in (1, 3, 2):
-            sends[jy, jx].wait_recv()
-            total = total + inbox_x[jy, jx - 1].astype(jnp.float32)
-        if jy:
-            relay_y[jy - 1] = total.astype(jnp.bfloat16)
-            onward[jy] = push(
-                relay_y.at[jy - 1], inbox_y.at[jy - 1], send_py.at[jy - 1], recv_py.at[jy - 1], {"rep": y_peer(jy)}
-            )
-    for jy in (1, 3, 2):
-        onward[jy].wait_recv()
-        total = total + inbox_y[jy - 1].astype(jnp.float32)
+    for jy in range(NY):
+        for jx in range(NX):
+            outbox[jy, jx] = partial_of(((yh + jy) % NY) * NX + (x + jx) % NX)
+    upper, lower = pl.ds(0, X_FIRST), pl.ds(X_FIRST, 128 - X_FIRST)
+    hops = (2, 1, 3, 0)
+    by_x, by_y = {}, {}
+    for j in hops:
+        for step in hops[:3]:
+            by_x[j, step] = push(
+                outbox.at[j, step, upper], inbox_x.at[j, step - 1],
+                send_px.at[j, step - 1], recv_px.at[j, step - 1], {"rep": x_peer(step)},
+            )
+        for step in hops[:3]:
+            by_y[j, step] = push(
+                outbox.at[step, j, lower], inbox_q.at[j, step - 1],
+                send_pq.at[j, step - 1], recv_pq.at[j, step - 1], {"rep": y_peer(step)},
+            )
+    then_y, then_x = {}, {}
+    for j in hops:
+        total = outbox[j, 0, upper].astype(jnp.float32)
+        for step in (1, 3, 2):
+            by_x[j, step].wait_recv()
+            total = total + inbox_x[j, step - 1].astype(jnp.float32)
+        if j:
+            relay_y[j - 1] = total.astype(jnp.bfloat16)
+            then_y[j] = push(
+                relay_y.at[j - 1], inbox_y.at[j - 1], send_py.at[j - 1], recv_py.at[j - 1], {"rep": y_peer(j)}
+            )
+        under = outbox[0, j, lower].astype(jnp.float32)
+        for step in (1, 3, 2):
+            by_y[j, step].wait_recv()
+            under = under + inbox_q[j, step - 1].astype(jnp.float32)
+        if j:
+            relay_x[j - 1] = under.astype(jnp.bfloat16)
+            then_x[j] = push(
+                relay_x.at[j - 1], inbox_r.at[j - 1], send_pr.at[j - 1], recv_pr.at[j - 1], {"rep": x_peer(j)}
+            )
+    for j in (1, 3, 2):
+        then_x[j].wait_recv()
+        under = under + inbox_r[j - 1].astype(jnp.float32)
+    for j in (1, 3, 2):
+        then_y[j].wait_recv()
+        total = total + inbox_y[j - 1].astype(jnp.float32)
+    total = jnp.concatenate([total, under], axis=0)
     high = total.astype(jnp.bfloat16)
     low = (total - high.astype(jnp.float32)).astype(jnp.bfloat16)
     hidden = jnp.dot(high, weight[...], preferred_element_type=jnp.float32)
@@ -195,9 +216,12 @@
             pltpu.VMEM((8, 128), jnp.int32),
             pltpu.SMEM((8, 128), jnp.int32),
             pltpu.VMEM((NY, NX, 128, 128), bf16),
-            pltpu.VMEM((NY, NX - 1, 128, 128), bf16),
-            pltpu.VMEM((NY - 1, 128, 128), bf16),
-            pltpu.VMEM((NY - 1, 128, 128), bf16),
+            pltpu.VMEM((NY, NX - 1, X_FIRST, 128), bf16),
+            pltpu.VMEM((NY - 1, X_FIRST, 128), bf16),
+            pltpu.VMEM((NY - 1, X_FIRST, 128), bf16),
+            pltpu.VMEM((NX, NY - 1, 128 - X_FIRST, 128), bf16),
+            pltpu.VMEM((NX - 1, 128 - X_FIRST, 128), bf16),
+            pltpu.VMEM((NX - 1, 128 - X_FIRST, 128), bf16),
             dma((8,)),
             dma((NZ,)),
             dma((NZ,)),
@@ -209,6 +233,10 @@
             dma((NY, NX - 1)),
             dma((NY - 1,)),
             dma((NY - 1,)),
+            dma((NX, NY - 1)),
+            dma((NX, NY - 1)),
+            dma((NX - 1,)),
+            dma((NX - 1,)),
         ],
         compiler_params=pltpu.CompilerParams(
             collective_id=0, has_side_effects=True, vmem_limit_bytes=60 * 1024 * 1024

time: 43 us -> 42.1 us (0.979)
  Pallas kernels: 40.7 us -> 39.8 us
    pallas_call x1, Pallas kernels: 40.7 us -> 39.8 us  [shards(): pl.pallas_call(kernel, out_shape=jax.ShapeDtypeStruct((128, 256), bf16),...]
where the time goes in v3:
time: 42.1 us; the launch traced here: 41.9 us
  Pallas kernels  39.8 us (95%)
  local copies, waits for them, and re-layouts  1.47 us (3%)
  between operations  0.66 us (2%)
    pallas_call x1, Pallas kernels, shards(): pl.pallas_call(kernel, out_shape=jax.ShapeDtypeStruct((128, 256), bf16),...  39.8 us
    unnamed x1, local copies, waits for them, and re-layouts  1.47 us

profile of v3, /device:TPU:1, one launch (start us, length us, event | category | flops | bytes accessed | tf_op | source)
XLA Modules:
  0.0 41.9 jit_solution(9564449577127769391)
XLA Ops:
  0.7 39.8 %layer.1 = bf16[128,256]{1,0:T(8,128)(2,1)} custom-call(bf16[128,128]{1,0:T(8,128)(2,1)} %features.1, bf16[128,128,128]{2,1,0:T(8,128)(2,1)} %adjacency.1, s32[1,128]{1,0:T(1,128)} %bitcast.6, s32[1,128]{1,0:T(1,128)} %bitcast.7, s32[1,1]{1,0:T(1,128)} %bitcast.4.count_in, bf16[128,256]{1,0:T(8,128)(2,1)} %weight_in.1, f32[1,256]{1,0:T(1,128)} %bitcast.5), custom_call_target="tpu_custom_call" | custom-call | flops 536870912 | bytes 4194304 | tf_op jit(solution)/shard_map/layer/pallas_call | solution.py:202
  40.4 1.5 %copy.10 = bf16[128,256]{1,0:T(8,128)(2,1)} copy(bf16[128,256]{1,0:T(8,128)(2,1)} %layer.1) | data formatting | bytes 131072

commit v4 on v3

--- a/solution.py
+++ b/solution.py
@@ -7,13 +7,13 @@
 
 MESH = pl.DeviceIdType.MESH
 NX, NY, NZ = 4, 4, 8
-X_FIRST = 96
+X_FIRST = 80
 PAIRS = 72
 
 
 def kernel(
-    features, adjacency, rows_in, cols_in, count_in, weight_in, bias_in, out_ref,
-    rows_ref, cols_ref, count_ref, weight, bias,
+    features, adjacency, rows_in, cols_in, count_in, out_ref,
+    rows_ref, cols_ref, count_ref,
     slab, tiles, sums, plan_v, plan, outbox, inbox_x, relay_y, inbox_y, inbox_q, relay_x, inbox_r,
     local_sem, send_z, recv_z, send_y, recv_y, send_c, recv_c, send_px, recv_px, send_py, recv_py,
     send_pq, recv_pq, send_pr, recv_pr,
@@ -36,10 +36,17 @@
     def block(owner):
         return slab.at[owner + 1]
 
+    barrier = pltpu.get_barrier_semaphore()
+    for peer in [at_z(step) for step in (4, 3, 5, 2, 6, 1, 7)] + [partner, sibling]:
+        pl.semaphore_signal(barrier, inc=1, device_id={"section": peer}, device_id_type=MESH)
+    for step in range(1, NX):
+        pl.semaphore_signal(barrier, inc=1, device_id={"rep": x_peer(step)}, device_id_type=MESH)
+    for step in range(1, NY):
+        pl.semaphore_signal(barrier, inc=1, device_id={"rep": y_peer(step)}, device_id_type=MESH)
     small = [
         pltpu.make_async_copy(source, target, local_sem.at[3 + i])
         for i, (source, target) in enumerate(
-            ((rows_in, rows_ref), (cols_in, cols_ref), (count_in, count_ref), (weight_in, weight), (bias_in, bias))
+            ((rows_in, rows_ref), (cols_in, cols_ref), (count_in, count_ref))
         )
     ]
     tile_copy = pltpu.make_async_copy(adjacency, tiles, local_sem.at[0])
@@ -49,17 +56,10 @@
         copy.start()
     tile_copy.start()
 
-    barrier = pltpu.get_barrier_semaphore()
-    for peer in [at_z(step) for step in range(1, NZ)] + [partner, sibling]:
-        pl.semaphore_signal(barrier, inc=1, device_id={"section": peer}, device_id_type=MESH)
-    for step in range(1, NX):
-        pl.semaphore_signal(barrier, inc=1, device_id={"rep": x_peer(step)}, device_id_type=MESH)
-    for step in range(1, NY):
-        pl.semaphore_signal(barrier, inc=1, device_id={"rep": y_peer(step)}, device_id_type=MESH)
     own_copy.wait()
     pl.semaphore_wait(barrier, NZ + 1 + NX - 1 + NY - 1)
 
-    sent = []
+    sent = [[]]
 
     def push(source, target, send, recv, peer):
         copy = pltpu.make_async_remote_copy(
@@ -67,7 +67,7 @@
             device_id=peer, device_id_type=MESH,
         )
         copy.start()
-        sent.append(copy)
+        sent[-1].append(copy)
         return copy
 
     def along_z(step):
@@ -135,7 +135,7 @@
         sums[k] = total
         return total, row
 
-    lax.fori_loop(0, PAIRS, step_of, (jnp.zeros((128, 128), jnp.float32), jnp.int32(-1)), unroll=24)
+    lax.fori_loop(0, PAIRS, step_of, (jnp.zeros((128, 128), jnp.float32), jnp.int32(-1)), unroll=36)
 
     def partial_of(q):
         end = jnp.maximum((plan[2, q] >> 1) - 1, 0)
@@ -146,6 +146,8 @@
             outbox[jy, jx] = partial_of(((yh + jy) % NY) * NX + (x + jx) % NX)
     upper, lower = pl.ds(0, X_FIRST), pl.ds(X_FIRST, 128 - X_FIRST)
     hops = (2, 1, 3, 0)
+    gathered = sent[0]
+    sent.append([])
     by_x, by_y = {}, {}
     for j in hops:
         for step in hops[:3]:
@@ -158,6 +160,8 @@
                 outbox.at[step, j, lower], inbox_q.at[j, step - 1],
                 send_pq.at[j, step - 1], recv_pq.at[j, step - 1], {"rep": y_peer(step)},
             )
+    for copy in gathered:
+        copy.wait_send()
     then_y, then_x = {}, {}
     for j in hops:
         total = outbox[j, 0, upper].astype(jnp.float32)
@@ -185,12 +189,8 @@
         then_y[j].wait_recv()
         total = total + inbox_y[j - 1].astype(jnp.float32)
     total = jnp.concatenate([total, under], axis=0)
-    high = total.astype(jnp.bfloat16)
-    low = (total - high.astype(jnp.float32)).astype(jnp.bfloat16)
-    hidden = jnp.dot(high, weight[...], preferred_element_type=jnp.float32)
-    hidden = hidden + jnp.dot(low, weight[...], preferred_element_type=jnp.float32)
-    out_ref[...] = jnp.maximum(hidden + bias[...], 0.0).astype(jnp.bfloat16)
-    for copy in sent:
+    out_ref[...] = total.astype(jnp.bfloat16)
+    for copy in sent[1]:
         copy.wait_send()
 
 
@@ -199,17 +199,15 @@
     anywhere = pl.BlockSpec(memory_space=pl.ANY)
     dma = pltpu.SemaphoreType.DMA
     bf16 = jnp.bfloat16
-    return pl.pallas_call(
+    summed = pl.pallas_call(
         kernel,
-        out_shape=jax.ShapeDtypeStruct((128, 256), bf16),
-        in_specs=[anywhere] * 7,
+        out_shape=jax.ShapeDtypeStruct((128, 128), bf16),
+        in_specs=[anywhere] * 5,
         out_specs=vmem,
         scratch_shapes=[
             pltpu.VMEM((1, 128), jnp.int32),
             pltpu.VMEM((1, 128), jnp.int32),
             pltpu.VMEM((1, 1), jnp.int32),
-            pltpu.VMEM((128, 256), bf16),
-            pltpu.VMEM((1, 256), jnp.float32),
             pltpu.VMEM((4 * NZ + 1, 128, 128), bf16),
             pltpu.VMEM((128, 128, 128), bf16),
             pltpu.VMEM((PAIRS, 128, 128), jnp.float32),
@@ -243,7 +241,9 @@
         ),
         cost_estimate=pl.CostEstimate(flops=2 * 128**4, bytes_accessed=128**3 * 2, transcendentals=0),
         name="layer",
-    )(features, adj_tiles, tile_rows.reshape(1, 128), tile_cols.reshape(1, 128), tile_counts.reshape(1, 1), weight, out_bias.reshape(1, 256))
+    )(features, adj_tiles, tile_rows.reshape(1, 128), tile_cols.reshape(1, 128), tile_counts.reshape(1, 1))
+    hidden = jnp.dot(summed, weight, preferred_element_type=jnp.float32)
+    return jnp.maximum(hidden + out_bias, 0.0).astype(bf16)
 
 
 def solution(mesh):

time: 42.1 us -> 41.7 us (level)
  matrix products: 0 us -> 1.54 us
  local copies, waits for them, and re-layouts: 1.47 us -> 0.01 us
  Pallas kernels: 39.8 us -> 39.2 us
    dot_general x0 -> x1, matrix products: none -> 1.54 us  [shards(): hidden = jnp.dot(summed, weight, preferred_element_type=jnp.float32)]
    unnamed x1 -> x4, local copies, waits for them, and re-layouts: 1.47 us -> 0.01 us
    pallas_call x1, Pallas kernels: 39.8 us -> 39.2 us  [shards(): pl.pallas_call(kernel, out_shape=jax.ShapeDtypeStruct((128, 128), bf16),...]
where the time goes in v4:
time: 41.7 us; the launch traced here: 41.5 us
  Pallas kernels  39.2 us (94%)
  matrix products  1.54 us (4%)
  between operations  0.71 us (2%)
    pallas_call x1, Pallas kernels, shards(): pl.pallas_call(kernel, out_shape=jax.ShapeDtypeStruct((128, 128), bf16),...  39.2 us
    dot_general x1, matrix products, shards(): hidden = jnp.dot(summed, weight, preferred_element_type=jnp.float32)  1.54 us

profile of v4, /device:TPU:1, one launch (start us, length us, event | category | flops | bytes accessed | tf_op | source)
XLA Modules:
  0.0 41.5 jit_solution(1739617812028986348)
XLA Ops:
  0.0 0.0 copy-start
  0.0 0.0 copy-start.1
  0.7 39.2 %layer.1 = bf16[128,128]{1,0:T(8,128)(2,1)} custom-call(bf16[128,128]{1,0:T(8,128)(2,1)} %features.1, bf16[128,128,128]{2,1,0:T(8,128)(2,1)} %adjacency.1, s32[1,128]{1,0:T(1,128)} %bitcast.6, s32[1,128]{1,0:T(1,128)} %bitcast.7, s32[1,1]{1,0:T(1,128)} %bitcast.5.count_in), custom_call_target="tpu_custom_call" | custom-call | flops 536870912 | bytes 4194304 | tf_op jit(solution)/shard_map/layer/pallas_call | solution.py:202
  39.9 0.0 copy-done
  39.9 0.0 copy-done.1
  39.9 1.5 %fusion.1 = bf16[128,256]{1,0:T(8,128)(2,1)} fusion(bf16[128,128]{1,0:T(8,128)(2,1)} %layer.1, bf16[128,256]{1,0:T(8,128)(2,1)S(1)} %copy-done, f32[256]{0:T(256)S(1)} %copy-done.1), kind=kOutput, calls=%fused_computation.2 | convolution fusion | flops 8486912 | bytes 164864 | tf_op jit(solution)/shard_map/dot_general | solution.py:245
Async XLA Ops:
  0.0 39.9 %copy-start = (bf16[128,256]{1,0:T(8,128)(2,1)S(1)}, bf16[128,256]{1,0:T(8,128)(2,1)}, u32[]{:S(2)}) copy-start(bf16[128,256]{1,0:T(8,128)(2,1)} %param.12) | copy-start | bytes 196612
  0.0 39.9 %copy-start.1 = (f32[256]{0:T(256)S(1)}, f32[256]{0:T(256)}, u32[]{:S(2)}) copy-start(f32[256]{0:T(256)} %param.13) | copy-start | bytes 3076

commit v5 on v4

--- a/solution.py
+++ b/solution.py
@@ -155,6 +155,7 @@
                 outbox.at[j, step, upper], inbox_x.at[j, step - 1],
                 send_px.at[j, step - 1], recv_px.at[j, step - 1], {"rep": x_peer(step)},
             )
+    for j in hops:
         for step in hops[:3]:
             by_y[j, step] = push(
                 outbox.at[step, j, lower], inbox_q.at[j, step - 1],

time: 41.7 us -> 41.7 us (level)
  no operation moved by 1% of the time
where the time goes in v5:
time: 41.7 us; the launch traced here: 41.5 us
  Pallas kernels  39.2 us (94%)
  matrix products  1.54 us (4%)
  between operations  0.71 us (2%)
    pallas_call x1, Pallas kernels, shards(): pl.pallas_call(kernel, out_shape=jax.ShapeDtypeStruct((128, 128), bf16),...  39.2 us
    dot_general x1, matrix products, shards(): hidden = jnp.dot(summed, weight, preferred_element_type=jnp.float32)  1.54 us

profile of v5, /device:TPU:1, one launch (start us, length us, event | category | flops | bytes accessed | tf_op | source)
XLA Modules:
  0.0 41.5 jit_solution(17043461992256077375)
XLA Ops:
  0.0 0.0 copy-start
  0.0 0.0 copy-start.1
  0.7 39.2 %layer.1 = bf16[128,128]{1,0:T(8,128)(2,1)} custom-call(bf16[128,128]{1,0:T(8,128)(2,1)} %features.1, bf16[128,128,128]{2,1,0:T(8,128)(2,1)} %adjacency.1, s32[1,128]{1,0:T(1,128)} %bitcast.6, s32[1,128]{1,0:T(1,128)} %bitcast.7, s32[1,1]{1,0:T(1,128)} %bitcast.5.count_in), custom_call_target="tpu_custom_call" | custom-call | flops 536870912 | bytes 4194304 | tf_op jit(solution)/shard_map/layer/pallas_call | solution.py:203
  39.9 0.0 copy-done
  39.9 0.0 copy-done.1
  39.9 1.5 %fusion.1 = bf16[128,256]{1,0:T(8,128)(2,1)} fusion(bf16[128,128]{1,0:T(8,128)(2,1)} %layer.1, bf16[128,256]{1,0:T(8,128)(2,1)S(1)} %copy-done, f32[256]{0:T(256)S(1)} %copy-done.1), kind=kOutput, calls=%fused_computation.2 | convolution fusion | flops 8486912 | bytes 164864 | tf_op jit(solution)/shard_map/dot_general | solution.py:246
Async XLA Ops:
  0.0 39.9 %copy-start = (bf16[128,256]{1,0:T(8,128)(2,1)S(1)}, bf16[128,256]{1,0:T(8,128)(2,1)}, u32[]{:S(2)}) copy-start(bf16[128,256]{1,0:T(8,128)(2,1)} %param.12) | copy-start | bytes 196612
  0.0 39.9 %copy-start.1 = (f32[256]{0:T(256)S(1)}, f32[256]{0:T(256)}, u32[]{:S(2)}) copy-start(f32[256]{0:T(256)} %param.13) | copy-start | bytes 3076
